TPU v7x, 768 devices: a whole 4x8x12 slice. The times are simulated.
768 devices in a mesh: vocab: 16 (over z_hi, x), dp: 48 (over z_lo, y, core).
Axes of the slice: x: 4, y: 8, z: 12 (z_hi: 4, z_lo: 3; z = z_hi * 3 + z_lo), core: 2. Of those that a mesh axis runs over, the one named last changes fastest.
Arguments:
- hidden: bfloat16 [30720, 2048], P('dp'), may hold values from -300 to 300
- head: bfloat16 [13824, 2048], P('vocab'), may hold values from -1 to 1
- targets: int32 [30720], P('dp'), may hold values from 0 to 13823
- mask_counts: int32 [192], P('dp'), may hold values from 20 to 160, as said below
- answer_lengths: int32 [192], P('dp'), may hold values from 20 to 640, as said below
Outputs:
- seq_loss: float32 [192], P('dp')
- head_grad: float32 [13824, 2048], P(('vocab', 'dp'))
Inputs may be any that keep to these rules, and one draw needn't show every extreme that they name: `mask_counts`: in each data group the counts sum to at most 640; in every draw some data group has all its counts equal to 160. `answer_lengths`: each sequence's length is at least its mask count and at most four times it.
All inputs are finite; a program needn't handle non-finite values.
Results may differ from a plain program's by a relative error of at most 0.0025.
Values sent between devices are 32-bit elements; how exact they have to be, the bound alone decides.
A program may use at most 64 MiB of HBM per device.

v0:
```python
import jax
import jax.numpy as jnp
from jax import lax
from jax.sharding import PartitionSpec as P


def row_weights(counts, lengths, row_count):
    position = jnp.arange(row_count, dtype=jnp.int32)
    seq_ends = jnp.cumsum(counts)
    member = jnp.sum((position[None, :] >= seq_ends[:, None]).astype(jnp.int32), axis=0)
    onehot_seq = (member[None, :] == jnp.arange(counts.shape[0], dtype=jnp.int32)[:, None]).astype(
        jnp.float32
    )
    inverse_rate = lengths.astype(jnp.float32) / counts.astype(jnp.float32)
    weights = jnp.dot(inverse_rate, onehot_seq, precision=lax.Precision.HIGHEST)
    return (onehot_seq, weights)


def on_device(hidden, head, targets, mask_counts, answer_lengths):
    vocab_rows = head.shape[0]
    row_count = hidden.shape[0]
    start_row = lax.axis_index("vocab") * vocab_rows
    logits = lax.dot_general(
        head, hidden, (((1,), (1,)), ((), ())), preferred_element_type=jnp.float32
    )
    local_ids = jnp.arange(vocab_rows, dtype=jnp.int32)[:, None] + start_row
    target_hit = local_ids == targets[None, :]
    target_logit = jnp.sum(jnp.where(target_hit, logits, jnp.float32(0.0)), axis=0)
    local_peak = jnp.max(logits, axis=0)
    peak = lax.pmax(local_peak, "vocab")
    partial_exp = jnp.sum(jnp.exp(logits - peak[None, :]), axis=0)
    total_exp, target_total = lax.psum((partial_exp, target_logit), "vocab")
    log_total = peak + jnp.log(total_exp)
    cross = log_total - target_total
    onehot_seq, weights = row_weights(mask_counts, answer_lengths, row_count)
    seq_loss = jnp.dot(onehot_seq, cross, precision=lax.Precision.HIGHEST) / mask_counts.astype(
        jnp.float32
    )
    probability = jnp.exp(logits - log_total[None, :])
    grad_rows = ((probability - target_hit.astype(jnp.float32)) * weights[None, :]).astype(
        jnp.bfloat16
    )
    partial_grad = jnp.dot(grad_rows, hidden, preferred_element_type=jnp.float32)
    head_grad = lax.psum_scatter(partial_grad, "dp", scatter_dimension=0, tiled=True)
    return (seq_loss, head_grad)


def solution(mesh):
    return jax.shard_map(
        on_device,
        mesh=mesh,
        in_specs=(P("dp", None), P("vocab", None), P("dp"), P("dp"), P("dp")),
        out_specs=(P("dp"), P(("vocab", "dp"), None)),
        check_vma=False,
    )
```

profile of v0, /device:TPU:562, one launch (start us, length us, event | category | flops | bytes accessed | tf_op | source)
XLA Modules:
  0.0 372.2 jit_solution(9701512206676667840)
XLA Ops:
  0.7 2.0 copy-done
  2.6 6.1 %fusion.17 = (f32[640]{0:T(1024)S(1)}, f32[864,640]{1,0:T(8,128)}) fusion(bf16[864,2048]{1,0:T(8,128)(2,1)S(1)} %copy-done, bf16[640,2048]{1,0:T(8,128)(2,1)} %param.5), kind=kOutput, calls=%fused_computation.26 | convolution fusion | flops 2265476608 | bytes 8374784 | tf_op jit(solution)/shard_map/dot_general | solution.py:23
  8.8 43.2 %pmax.7 = f32[640]{0:T(1024)S(1)} all-reduce(f32[640]{0:T(1024)S(1)} %get-tuple-element.8), channel_id=1, replica_groups=mesh['vocab'=16,'dp'=48] {'vocab'}, use_global_device_ids=true, to_apply=%region_3.4 | all-reduce | flops 640 | bytes 5120 | tf_op jit(solution)/shard_map/pmax | solution.py:30
  52.1 0.7 convert_reduce_fusion
  52.8 2.1 fusion.1
  55.0 46.2 %all-reduce.2 = (f32[640]{0:T(1024)}, f32[640]{0:T(1024)}) all-reduce(f32[640]{0:T(1024)S(1)} %get-tuple-element.3, f32[640]{0:T(1024)S(1)} %get-tuple-element.2), channel_id=1, replica_groups=mesh['vocab'=16,'dp'=48] {'vocab'}, use_global_device_ids=true, to_apply=%region_5.6 | all-reduce | flops 1280 | bytes 10240 | tf_op jit(solution)/shard_map/psum | solution.py:32
  101.2 0.7 fusion.16
  101.9 0.9 convolution_reduce_fusion
  102.8 8.4 %fusion.5 = f32[864,2048]{1,0:T(8,128)} fusion(bf16[640,2048]{1,0:T(8,128)(2,1)} %param.5, f32[864,640]{1,0:T(8,128)} %get-tuple-element.9, f32[640]{0:T(1024)S(1)} %convolution_reduce_fusion, f32[640]{0:T(1024)S(1)} %get-tuple-element.7, s32[640]{0:T(1024)} %param.7, s32[864]{0:T(1024)S(1)} %iota_add_fusion), kind=kOutput, calls=%fused_computation.9 | convolution fusion | flops 2268241920 | bytes 11922304 | tf_op jit(solution)/shard_map/dot_general | solution.py:43
  111.2 112.6 %fusion = f32[24,2048]{1,0:T(8,128)} fusion(f32[864,2048]{1,0:T(8,128)} %fusion.5), kind=kCustom, calls=%all-reduce-scatter | all-reduce-scatter fusion | flops 2359297 | bytes 7278592
  223.8 1.3 collective-permute-start.10
  225.1 0.9 slice
  226.0 1.3 collective-permute-start.11
  227.3 1.3 collective-permute-start.9
  228.6 1.3 collective-permute-start.8
  229.9 1.3 collective-permute-start.7
  231.2 28.7 %collective-permute-done.11 = f32[18,2048]{1,0:T(8,128)} collective-permute-done((f32[18,2048]{1,0:T(8,128)S(1)}, f32[18,2048]{1,0:T(8,128)}, u32[]{:S(2)}, u32[]{:S(2)}) %collective-permute-start.11) | collective-permute-done | bytes 147488
  260.0 1.3 collective-permute-start.6
  261.3 1.3 collective-permute-start.5
  262.6 1.3 dynamic-slice.4
  264.5 7.0 %collective-permute-done.9 = f32[24,2048]{1,0:T(8,128)} collective-permute-done((f32[24,2048]{1,0:T(8,128)}, f32[24,2048]{1,0:T(8,128)}, u32[]{:S(2)}, u32[]{:S(2)}) %collective-permute-start.9) | collective-permute-done | bytes 196640
  271.5 1.3 collective-permute-start.4
  272.8 6.9 %collective-permute-done.8 = f32[24,2048]{1,0:T(8,128)} collective-permute-done((f32[24,2048]{1,0:T(8,128)}, f32[24,2048]{1,0:T(8,128)}, u32[]{:S(2)}, u32[]{:S(2)}) %collective-permute-start.8) | collective-permute-done | bytes 196640
  279.7 1.3 collective-permute-start.3
  281.0 1.9 collective-permute-start.2
  283.0 7.0 %collective-permute-start.1 = (f32[24,2048]{1,0:T(8,128)}, f32[24,2048]{1,0:T(8,128)}, u32[]{:S(2)}, u32[]{:S(2)}) collective-permute-start(f32[24,2048]{1,0:T(8,128)} %fusion), channel_id=1, source_target_pairs={{0,2},{1,3},{2,4},{3,5},{4,6},{5,7},{6,8},{7,9},{8,10},{9,11},{10,... | collective-permute-start | bytes 589832
  290.0 22.2 %collective-permute-done.5 = f32[24,2048]{1,0:T(8,128)} collective-permute-done((f32[24,2048]{1,0:T(8,128)}, f32[24,2048]{1,0:T(8,128)}, u32[]{:S(2)}, u32[]{:S(2)}) %collective-permute-start.5) | collective-permute-done | bytes 196640
  312.2 7.5 %collective-permute-start = (f32[24,2048]{1,0:T(8,128)}, f32[24,2048]{1,0:T(8,128)}, u32[]{:S(2)}, u32[]{:S(2)}) collective-permute-start(f32[24,2048]{1,0:T(8,128)} %fusion), channel_id=1, source_target_pairs={{0,1},{1,2},{2,3},{3,4},{4,5},{5,6},{6,7},{7,8},{8,9},{9,10},{10,1... | collective-permute-start | bytes 589832
  320.4 12.9 %collective-permute-done.3 = f32[24,2048]{1,0:T(8,128)} collective-permute-done((f32[24,2048]{1,0:T(8,128)}, f32[24,2048]{1,0:T(8,128)}, u32[]{:S(2)}, u32[]{:S(2)}) %collective-permute-start.3) | collective-permute-done | bytes 196640
  333.3 15.1 %collective-permute-done.1 = f32[24,2048]{1,0:T(8,128)} collective-permute-done((f32[24,2048]{1,0:T(8,128)}, f32[24,2048]{1,0:T(8,128)}, u32[]{:S(2)}, u32[]{:S(2)}) %collective-permute-start.1) | collective-permute-done | bytes 196640
  348.4 22.1 %concatenate = f32[306,2048]{1,0:T(8,128)} concatenate(f32[18,2048]{1,0:T(8,128)} %collective-permute-done.11, f32[24,2048]{1,0:T(8,128)} %collective-permute-done.10, f32[24,2048]{1,0:T(8,128)} %collective-permute-done.9, f32[24,2048]{1,0:T(8,128)} %collective-permute-done.8, f32[24,2048]{1,0:T(8,128)} %collective-permute-done.7, f32[24,2048]{1,0:T(8,128)} %collective-permute-done.6, ...), dimensions={0} | concatenate | bytes 5013504
  370.6 1.6 constant_dynamic-slice_fusion
  (17 shorter events, 1.0 us)
Async XLA Ops:
  0.6 2.0 copy-start
  2.6 49.3 %copy-start.2 = (s32[4]{0:T(128)S(1)}, s32[4]{0:T(128)}, u32[]{:S(2)}) copy-start(s32[4]{0:T(128)} %param.8) | copy-start | bytes 52
  111.2 208.4 %copy-start.1 = (s32[640]{0:T(1024)S(1)}, s32[640]{0:T(1024)}, u32[]{:S(2)}) copy-start(s32[640]{0:T(1024)} %convert_reduce_fusion) | copy-start | bytes 7684
  111.2 208.5 %copy-start.3 = (s32[4]{0:T(128)S(1)}, s32[4]{0:T(128)}, u32[]{:S(2)}) copy-start(s32[4]{0:T(128)} %param.8) | copy-start | bytes 52
  223.8 37.5 %collective-permute-start.10 = (f32[24,2048]{1,0:T(8,128)}, f32[24,2048]{1,0:T(8,128)}, u32[]{:S(2)}, u32[]{:S(2)}) collective-permute-start(f32[24,2048]{1,0:T(8,128)} %fusion), channel_id=1, source_target_pairs={{0,11},{1,12},{2,13},{3,14},{4,15},{5,16},{6,17},{7,18},{8,19},{9,... | collective-permute-start | bytes 589832
  226.0 33.9 %collective-permute-start.11 = (f32[18,2048]{1,0:T(8,128)S(1)}, f32[18,2048]{1,0:T(8,128)}, u32[]{:S(2)}, u32[]{:S(2)}) collective-permute-start(f32[18,2048]{1,0:T(8,128)S(1)} %slice), channel_id=1, source_target_pairs={{0,12},{1,13},{2,14},{3,15},{4,16},{5,17},{6,18},{7,19},{8,20},{9,... | collective-permute-start | bytes 442376
  227.3 44.2 %collective-permute-start.9 = (f32[24,2048]{1,0:T(8,128)}, f32[24,2048]{1,0:T(8,128)}, u32[]{:S(2)}, u32[]{:S(2)}) collective-permute-start(f32[24,2048]{1,0:T(8,128)} %fusion), channel_id=1, source_target_pairs={{0,10},{1,11},{2,12},{3,13},{4,14},{5,15},{6,16},{7,17},{8,18},{9,... | collective-permute-start | bytes 589832
  228.6 51.1 %collective-permute-start.8 = (f32[24,2048]{1,0:T(8,128)}, f32[24,2048]{1,0:T(8,128)}, u32[]{:S(2)}, u32[]{:S(2)}) collective-permute-start(f32[24,2048]{1,0:T(8,128)} %fusion), channel_id=1, source_target_pairs={{0,9},{1,10},{2,11},{3,12},{4,13},{5,14},{6,15},{7,16},{8,17},{9,1... | collective-permute-start | bytes 589832
  229.9 51.1 %collective-permute-start.7 = (f32[24,2048]{1,0:T(8,128)}, f32[24,2048]{1,0:T(8,128)}, u32[]{:S(2)}, u32[]{:S(2)}) collective-permute-start(f32[24,2048]{1,0:T(8,128)} %fusion), channel_id=1, source_target_pairs={{0,8},{1,9},{2,10},{3,11},{4,12},{5,13},{6,14},{7,15},{8,16},{9,17... | collective-permute-start | bytes 589832
  260.0 23.0 %collective-permute-start.6 = (f32[24,2048]{1,0:T(8,128)}, f32[24,2048]{1,0:T(8,128)}, u32[]{:S(2)}, u32[]{:S(2)}) collective-permute-start(f32[24,2048]{1,0:T(8,128)} %fusion), channel_id=1, source_target_pairs={{0,7},{1,8},{2,9},{3,10},{4,11},{5,12},{6,13},{7,14},{8,15},{9,16}... | collective-permute-start | bytes 589832
  261.3 50.9 %collective-permute-start.5 = (f32[24,2048]{1,0:T(8,128)}, f32[24,2048]{1,0:T(8,128)}, u32[]{:S(2)}, u32[]{:S(2)}) collective-permute-start(f32[24,2048]{1,0:T(8,128)} %fusion), channel_id=1, source_target_pairs={{0,6},{1,7},{2,8},{3,9},{4,10},{5,11},{6,12},{7,13},{8,14},{9,15},... | collective-permute-start | bytes 589832
  271.5 48.8 %collective-permute-start.4 = (f32[24,2048]{1,0:T(8,128)}, f32[24,2048]{1,0:T(8,128)}, u32[]{:S(2)}, u32[]{:S(2)}) collective-permute-start(f32[24,2048]{1,0:T(8,128)} %fusion), channel_id=1, source_target_pairs={{0,5},{1,6},{2,7},{3,8},{4,9},{5,10},{6,11},{7,12},{8,13},{9,14},{... | collective-permute-start | bytes 589832
  279.7 53.5 %collective-permute-start.3 = (f32[24,2048]{1,0:T(8,128)}, f32[24,2048]{1,0:T(8,128)}, u32[]{:S(2)}, u32[]{:S(2)}) collective-permute-start(f32[24,2048]{1,0:T(8,128)} %fusion), channel_id=1, source_target_pairs={{0,4},{1,5},{2,6},{3,7},{4,8},{5,9},{6,10},{7,11},{8,12},{9,13},{1... | collective-permute-start | bytes 589832
  281.0 52.2 %collective-permute-start.2 = (f32[24,2048]{1,0:T(8,128)}, f32[24,2048]{1,0:T(8,128)}, u32[]{:S(2)}, u32[]{:S(2)}) collective-permute-start(f32[24,2048]{1,0:T(8,128)} %fusion), channel_id=1, source_target_pairs={{0,3},{1,4},{2,5},{3,6},{4,7},{5,8},{6,9},{7,10},{8,11},{9,12},{10... | collective-permute-start | bytes 589832
  283.0 65.4 %collective-permute-start.1 = (f32[24,2048]{1,0:T(8,128)}, f32[24,2048]{1,0:T(8,128)}, u32[]{:S(2)}, u32[]{:S(2)}) collective-permute-start(f32[24,2048]{1,0:T(8,128)} %fusion), channel_id=1, source_target_pairs={{0,2},{1,3},{2,4},{3,5},{4,6},{5,7},{6,8},{7,9},{8,10},{9,11},{10,... | collective-permute-start | bytes 589832
  312.2 36.2 %collective-permute-start = (f32[24,2048]{1,0:T(8,128)}, f32[24,2048]{1,0:T(8,128)}, u32[]{:S(2)}, u32[]{:S(2)}) collective-permute-start(f32[24,2048]{1,0:T(8,128)} %fusion), channel_id=1, source_target_pairs={{0,1},{1,2},{2,3},{3,4},{4,5},{5,6},{6,7},{7,8},{8,9},{9,10},{10,1... | collective-permute-start | bytes 589832
where the time goes:
time: 373 us; the launch traced here: 372 us
  blocking collectives  202 us (54%)
  waiting for transfers between devices  92.9 us (25%)
  local copies, waits for them, and re-layouts  28 us (8%)
  starting transfers between devices  28 us (8%)
  matrix products  16.1 us (4%)
    unnamed x1, blocking collectives  113 us
    unnamed x12, waiting for transfers between devices  92.9 us
    psum x1, blocking collectives, on_device(): total_exp, target_total = lax.psum((partial_exp, target_logit), 'vocab')  46.2 us
    pmax x1, blocking collectives, on_device(): peak = lax.pmax(local_peak, 'vocab')  43.2 us
    unnamed x12, local copies, waits for them, and re-layouts  28 us
    unnamed x12, starting transfers between devices  28 us
    dot_general x1, matrix products, on_device(): jnp.dot(grad_rows, hidden, preferred_element_type=jnp.float32)  8.45 us
  transfers between devices with their start and end apart: 12, of which 7 were waited for; matrix products, arithmetic and copies ran while one was open for 1% of the time, Pallas kernels for 0%

commit v1 on v0

v1 whole, which is shorter than its diff:
```python
import jax
import jax.numpy as jnp
from jax import lax
from jax.experimental import pallas as pl
from jax.experimental.pallas import tpu as pltpu
from jax.sharding import PartitionSpec as P

MESH = pl.DeviceIdType.MESH
F32 = jnp.float32

VOCAB_DEVS = 16
NZ, NY, NC = 3, 8, 2
LANES = 128
ROWS_A = 176
DISTANCES = (4, 3, 5, 2, 6, 1, 7, 0)


def kernel(hidden, head, targets, counts, lengths, out, loss,
           logits, probs, grad, stats, hits,
           core_in, ya0, ya, za, yb0, yb, zb, last,
           lse_s, lse_r, hit_s, hit_r, core_s, core_r,
           ya_s, ya_r, za_s, za_r, yb_s, yb_r, zb_s, zb_r):
    vocab_rows, width = head.shape
    slots = hidden.shape[0]
    block = vocab_rows * width // LANES // (NZ * NY * NC)
    pitch = width // LANES
    rows_b = block - ROWS_A
    half_a, half_b = ROWS_A // 2, rows_b // 2

    v = lax.axis_index("vocab")
    d = lax.axis_index("dp")
    c = d % NC
    y = (d // NC) % NY
    z = d // (NC * NY)

    partner = d + 1 - 2 * c
    y_next = [(z * NY + (y + 1) % NY) * NC + c, (z * NY + (y + NY - 1) % NY) * NC + c]
    z_peer = [(((z + k) % NZ) * NY + y) * NC + c for k in (1, 2)]
    v_peer = [(v + s) % VOCAB_DEVS for s in range(1, VOCAB_DEVS)]

    barrier = pltpu.get_barrier_semaphore()
    for peer in v_peer:
        pl.semaphore_signal(barrier, inc=1, device_id={"vocab": peer}, device_id_type=MESH)
    for peer in [partner] + y_next + z_peer:
        pl.semaphore_signal(barrier, inc=1, device_id={"dp": peer}, device_id_type=MESH)

    position = lax.broadcasted_iota(jnp.int32, (1, slots), 1)
    seqs = counts.shape[0]
    member = []
    begin = jnp.int32(0)
    weight = jnp.zeros((1, slots), F32)
    for k in range(seqs):
        end = begin + counts[k]
        inside = (position >= begin) & (position < end)
        member.append(inside)
        rate = jnp.full((1, slots), lengths[k], jnp.int32).astype(F32) / jnp.full(
            (1, slots), counts[k], jnp.int32
        ).astype(F32)
        weight = jnp.where(inside, rate, weight)
        begin = end

    part = vocab_rows // 3

    @pl.loop(0, 3)
    def _(i):
        rows = pl.ds(pl.multiple_of(i * part, part), part)
        logits[rows, :] = lax.dot_general(
            head[rows, :], hidden[...], (((1,), (1,)), ((), ())), preferred_element_type=F32
        )

    relative = targets[...] - v * vocab_rows
    tile = 96
    peak = jnp.full((8, slots), -jnp.inf, F32)
    target_sum = jnp.zeros((8, slots), F32)

    def first_pass(i, carry):
        peak, total = carry
        for k in range(tile // 8):
            at = pl.multiple_of(i * tile + k * 8, 8)
            value = logits[pl.ds(at, 8), :]
            ids = lax.broadcasted_iota(jnp.int32, (8, slots), 0) + at
            peak = jnp.maximum(peak, value)
            total = total + jnp.where(ids == relative, value, 0.0)
        return peak, total

    peak, target_sum = lax.fori_loop(0, vocab_rows // tile, first_pass, (peak, target_sum))
    peak = jnp.max(peak, axis=0, keepdims=True)
    hits[0] = jnp.sum(target_sum, axis=0, keepdims=True)

    def second_pass(i, total):
        for k in range(tile // 8):
            at = pl.multiple_of(i * tile + k * 8, 8)
            value = jnp.exp(logits[pl.ds(at, 8), :] - peak)
            logits[pl.ds(at, 8), :] = value
            total = total + value
        return total

    exp_sum = lax.fori_loop(0, vocab_rows // tile, second_pass, jnp.zeros((8, slots), F32))
    own_lse = peak + jnp.log(jnp.sum(exp_sum, axis=0, keepdims=True))
    stats[0] = own_lse

    pl.semaphore_wait(barrier, VOCAB_DEVS - 1 + 1 + 2 + 2)

    waits = []

    def send(src, dst, send_sem, recv_sem, axis, peer):
        copy = pltpu.make_async_remote_copy(
            src_ref=src, dst_ref=dst, send_sem=send_sem, recv_sem=recv_sem,
            device_id={axis: peer}, device_id_type=MESH,
        )
        copy.start()
        waits.append(copy)
        return copy

    lse_copies = [
        send(stats.at[0], stats.at[s], lse_s.at[s], lse_r.at[s], "vocab", v_peer[s - 1])
        for s in range(1, VOCAB_DEVS)
    ]
    hit_copies = [
        send(hits.at[0], hits.at[s], hit_s.at[s], hit_r.at[s], "vocab", v_peer[s - 1])
        for s in range(1, VOCAB_DEVS)
    ]
    for copy in lse_copies:
        copy.wait_recv()
    top = own_lse
    for s in range(1, VOCAB_DEVS):
        top = jnp.maximum(top, stats[s])
    total = jnp.exp(own_lse - top)
    for s in range(1, VOCAB_DEVS):
        total = total + jnp.exp(stats[s] - top)
    log_total = top + jnp.log(total)

    shift = jnp.exp(peak - log_total)

    @pl.loop(0, vocab_rows // 48)
    def _(i):
        for k in range(3):
            at = pl.multiple_of(i * 48 + k * 16, 16)
            ids = lax.broadcasted_iota(jnp.int32, (16, slots), 0) + at
            onehot = jnp.where(ids == relative, 1.0, 0.0)
            value = (logits[pl.ds(at, 16), :] * shift - onehot) * weight
            probs[pl.ds(at, 16), :] = value.astype(jnp.bfloat16)

    @pl.loop(0, width // 256)
    def _(n):
        columns = pl.ds(pl.multiple_of(n * 256, 256), 256)
        value = jnp.dot(probs[...], hidden[:, columns], preferred_element_type=F32)
        for j in range(2):
            grad[pl.ds(n * 2 + j, vocab_rows, stride=pitch), :] = value[:, j * LANES:(j + 1) * LANES]

    def line(zo, yo, co):
        return pl.multiple_of(((zo * NY + yo) * NC + co) * block, 8)

    def own(zo, yo, start, count):
        return pl.ds(pl.multiple_of(line(zo, yo, c) + start, 8), count)

    core_copies = {}
    for i, dist in enumerate(DISTANCES):
        yo = (y + dist) % NY
        for zo in range(NZ):
            at = i * NZ + zo
            core_copies[dist, zo] = send(
                grad.at[pl.ds(line(zo, yo, 1 - c), block)], core_in.at[at],
                core_s.at[at], core_r.at[at], "dp", partner,
            )

    zb_copies, ya_copies, yb_copies = {}, {}, {}

    def pair_sum(dist):
        yo = (y + dist) % NY
        i = DISTANCES.index(dist)
        for zo in range(NZ):
            core_copies[dist, zo].wait_recv()
            grad[own(zo, yo, 0, block), :] += core_in[i * NZ + zo]
        for k in range(2):
            zb_copies[dist, k] = send(
                grad.at[own((z + k + 1) % NZ, yo, ROWS_A, rows_b)], zb.at[k, dist],
                zb_s.at[k, dist], zb_r.at[k, dist], "dp", z_peer[k],
            )

    def owner(way, t):
        return (y + (4 - t if way == 0 else 4 + t)) % NY

    def step_a(t):
        if t > 0:
            for zo in range(NZ):
                for way in range(2):
                    ya_copies[way, t - 1, zo].wait_recv()
                    if t == 1:
                        grad[own(zo, owner(way, 1), way * half_a, half_a), :] += ya0[way, zo]
                    else:
                        grad[own(zo, owner(way, t), 0, ROWS_A), :] += ya[way, t - 2, zo]
                    if t < 4:
                        send_a(way, t, zo)
        else:
            for zo in range(NZ):
                for way in range(2):
                    send_a(way, 0, zo)

    def send_a(way, t, zo):
        if t == 0:
            src, dst = own(zo, owner(way, 0), way * half_a, half_a), ya0.at[way, zo]
        else:
            src, dst = own(zo, owner(way, t), 0, ROWS_A), ya.at[way, t - 1, zo]
        ya_copies[way, t, zo] = send(
            grad.at[src], dst, ya_s.at[way, t, zo], ya_r.at[way, t, zo], "dp", y_next[way]
        )

    def z_sum(dist):
        yo = (y + dist) % NY
        for k in range(2):
            zb_copies[dist, k].wait_recv()
        grad[own(z, yo, ROWS_A, rows_b), :] += zb[0, dist] + zb[1, dist]

    def step_b(t):
        for way in range(2):
            if t > 0:
                yb_copies[way, t - 1].wait_recv()
                if t == 1:
                    grad[own(z, owner(way, 1), ROWS_A + way * half_b, half_b), :] += yb0[way]
                else:
                    grad[own(z, owner(way, t), ROWS_A, rows_b), :] += yb[way, t - 2]
            if t == 0:
                src, dst = own(z, owner(way, 0), ROWS_A + way * half_b, half_b), yb0.at[way]
            elif t < 4:
                src, dst = own(z, owner(way, t), ROWS_A, rows_b), yb.at[way, t - 1]
            else:
                continue
            yb_copies[way, t] = send(
                grad.at[src], dst, yb_s.at[way, t], yb_r.at[way, t], "dp", y_next[way]
            )

    pair_sum(4)
    step_a(0)
    pair_sum(3)
    pair_sum(5)
    pair_sum(2)
    step_a(1)
    pair_sum(6)
    pair_sum(1)
    pair_sum(7)
    pair_sum(0)
    z_sum(4)
    step_b(0)
    step_a(2)
    z_sum(3)
    z_sum(5)
    step_b(1)
    step_a(3)
    z_sum(2)
    z_sum(6)
    step_b(2)
    z_sum(1)
    z_sum(7)
    step_b(3)
    step_a(4)
    za_copies = [
        send(grad.at[own((z + k + 1) % NZ, y, 0, ROWS_A)], za.at[k], za_s.at[k], za_r.at[k],
             "dp", z_peer[k])
        for k in range(2)
    ]
    z_sum(0)
    step_b(4)

    for copy in hit_copies:
        copy.wait_recv()
    target_logit = hits[0]
    for s in range(1, VOCAB_DEVS):
        target_logit = target_logit + hits[s]
    cross = log_total - target_logit
    for k in range(seqs):
        mean = jnp.where(member[k], cross, 0.0) / jnp.full((1, slots), counts[k], jnp.int32).astype(F32)
        loss[k] = jnp.sum(mean)

    last[pl.ds(ROWS_A, rows_b), :] = grad[own(z, y, ROWS_A, rows_b), :]
    for copy in za_copies:
        copy.wait_recv()
    last[pl.ds(0, ROWS_A), :] = grad[own(z, y, 0, ROWS_A), :] + za[0] + za[1]
    for j in range(pitch):
        out[:, j * LANES:(j + 1) * LANES] = last[pl.ds(j, out.shape[0], stride=pitch), :]

    for copy in waits:
        copy.wait_send()


def on_device(hidden, head, targets, mask_counts, answer_lengths):
    vocab_rows, width = head.shape
    slots = hidden.shape[0]
    lines = vocab_rows * width // LANES
    block = lines // (NZ * NY * NC)
    rows_b = block - ROWS_A
    vmem = pl.BlockSpec(memory_space=pltpu.VMEM)
    smem = pl.BlockSpec(memory_space=pltpu.SMEM)
    dma = pltpu.SemaphoreType.DMA
    head_grad, seq_loss = pl.pallas_call(
        kernel,
        out_shape=(
            jax.ShapeDtypeStruct((vocab_rows // (NZ * NY * NC), width), F32),
            jax.ShapeDtypeStruct(mask_counts.shape, F32),
        ),
        in_specs=[vmem, vmem, vmem, smem, smem],
        out_specs=(vmem, smem),
        scratch_shapes=[
            pltpu.VMEM((vocab_rows, slots), F32),
            pltpu.VMEM((vocab_rows, slots), jnp.bfloat16),
            pltpu.VMEM((lines, LANES), F32),
            pltpu.VMEM((VOCAB_DEVS, 1, slots), F32),
            pltpu.VMEM((VOCAB_DEVS, 1, slots), F32),
            pltpu.VMEM((NY * NZ, block, LANES), F32),
            pltpu.VMEM((2, NZ, ROWS_A // 2, LANES), F32),
            pltpu.VMEM((2, 3, NZ, ROWS_A, LANES), F32),
            pltpu.VMEM((2, ROWS_A, LANES), F32),
            pltpu.VMEM((2, rows_b // 2, LANES), F32),
            pltpu.VMEM((2, 3, rows_b, LANES), F32),
            pltpu.VMEM((2, NY, rows_b, LANES), F32),
            pltpu.VMEM((block, LANES), F32),
            dma((VOCAB_DEVS,)), dma((VOCAB_DEVS,)),
            dma((VOCAB_DEVS,)), dma((VOCAB_DEVS,)),
            dma((NY * NZ,)), dma((NY * NZ,)),
            dma((2, 4, NZ)), dma((2, 4, NZ)),
            dma((2,)), dma((2,)),
            dma((2, 4)), dma((2, 4)),
            dma((2, NY)), dma((2, NY)),
        ],
        compiler_params=pltpu.CompilerParams(
            collective_id=0, has_side_effects=True, vmem_limit_bytes=48 * 1024 * 1024
        ),
        cost_estimate=pl.CostEstimate(
            flops=4 * vocab_rows * slots * width,
            bytes_accessed=2 * (vocab_rows + slots) * width,
            transcendentals=vocab_rows * slots,
        ),
        name="head_gradient",
    )(hidden, head, targets.reshape(1, slots), mask_counts, answer_lengths)
    return seq_loss, head_grad


def solution(mesh):
    return jax.shard_map(
        on_device,
        mesh=mesh,
        in_specs=(P("dp", None), P("vocab", None), P("dp"), P("dp"), P("dp")),
        out_specs=(P("dp"), P(("vocab", "dp"), None)),
        check_vma=False,
    )
```

time: 373 us -> 75.8 us (0.20)
  the two profiles are of different devices: /device:TPU:562 before, /device:TPU:1 now
where the time goes in v1:
time: 75.8 us; the launch traced here: 75.6 us
  Pallas kernels  70 us (92%)
  local copies, waits for them, and re-layouts  4.93 us (7%)
    pallas_call x1, Pallas kernels, on_device(): pl.pallas_call(kernel, out_shape=(jax.ShapeDtypeStruct((vocab_rows // (NZ...  70 us
    unnamed x8, local copies, waits for them, and re-layouts  4.24 us

profile of v1, /device:TPU:1, one launch (start us, length us, event | category | flops | bytes accessed | tf_op | source)
XLA Modules:
  0.0 75.6 jit_solution(15211369078607672457)
XLA Ops:
  0.6 0.7 reshape.7.targets
  1.3 0.0 copy-start
  1.3 1.7 %copy-done = bf16[640,2048]{1,0:T(8,128)(2,1)S(1)} copy-done((bf16[640,2048]{1,0:T(8,128)(2,1)S(1)}, bf16[640,2048]{1,0:T(8,128)(2,1)}, u32[]{:S(2)}) %copy-start) | copy-done | bytes 2621464
  3.1 0.0 copy-start.1
  3.1 0.7 copy-done.1
  3.7 0.0 copy-start.2
  3.7 0.7 copy-done.2
  4.4 70.0 %head_gradient.1 = (f32[18,2048]{1,0:T(8,128)S(1)}, f32[4]{0:T(128)S(1)}) custom-call(bf16[640,2048]{1,0:T(8,128)(2,1)S(1)} %copy-done, bf16[864,2048]{1,0:T(8,128)(2,1)} %head.1, s32[1,640]{1,0:T(1,128)S(1)} %reshape.7.targets, s32[4]{0:T(128)S(1)} %copy-done.1, s32[4]{0:T(128)S(1)} %copy-done.2), custom_call_target="tpu_custom_call" | custom-call | flops 4529848320 | bytes 6160384 | tf_op jit(solution)/shard_map/head_gradient/pallas_call | solution.py:295
  74.4 0.5 copy.9
  74.9 0.7 copy.10
Async XLA Ops:
  1.3 1.7 %copy-start = (bf16[640,2048]{1,0:T(8,128)(2,1)S(1)}, bf16[640,2048]{1,0:T(8,128)(2,1)}, u32[]{:S(2)}) copy-start(bf16[640,2048]{1,0:T(8,128)(2,1)} %hidden.1) | copy-start | bytes 7864324
  3.1 0.7 copy-start.1
  3.7 0.7 copy-start.2

commit v2 on v0

v2 whole, which is shorter than its diff:
```python
import functools

import jax
import jax.numpy as jnp
from jax import lax
from jax.experimental import pallas as pl
from jax.experimental.pallas import tpu as pltpu
from jax.sharding import PartitionSpec as P

MESH = pl.DeviceIdType.MESH
F32 = jnp.float32

NX, NH = 4, 4
NZ, NY, NC = 3, 8, 2
LANES = 128
STEPS = 4
ROWS_A = 176
DISTANCES = (4, 3, 5, 2, 6, 1, 7, 0)


def toward(way, t):
    return (4 - t if way == 0 else 4 + t) % NY


ORDER = (
    ("product", 1), ("swap", 1, 4), ("product", 0), ("pair", 1, 4), ("swap", 0, 4), ("product", 2), ("swap", 2, 4),
    ("swap", 1, 5), ("pair", 0, 4), ("swap", 1, 3), ("swap", 1, 0), ("pair", 2, 4), ("pair", 1, 5), ("swap", 0, 5),
    ("swap", 0, 3), ("swap", 0, 6), ("swap", 0, 1), ("pair", 1, 3), ("a", 1, 1, 0), ("a", 1, 1, 1), ("swap", 2, 5),
    ("swap", 1, 7), ("swap", 2, 2), ("pair", 0, 3), ("a", 0, 1, 0), ("swap", 2, 6), ("swap", 1, 6), ("pair", 0, 5),
    ("swap", 2, 3), ("swap", 1, 1), ("a", 0, 1, 1), ("swap", 0, 7), ("zsum", 4), ("swap", 1, 2), ("pair", 2, 3),
    ("pair", 1, 1), ("pair", 0, 6), ("pair", 1, 6), ("pair", 1, 7), ("pair", 2, 5), ("a", 2, 1, 0), ("a", 2, 1, 1),
    ("swap", 2, 7), ("pair", 1, 2), ("a", 1, 2, 0), ("a", 1, 2, 1), ("pair", 0, 1), ("swap", 0, 0), ("pair", 2, 6),
    ("swap", 2, 1), ("zsum", 3), ("swap", 0, 2), ("pair", 0, 2), ("b", 1, 0), ("zsum", 5), ("pair", 0, 7),
    ("a", 0, 2, 1), ("b", 1, 1), ("a", 0, 2, 0), ("a", 2, 2, 1), ("a", 1, 3, 0), ("a", 1, 3, 1), ("pair", 2, 2),
    ("swap", 2, 0), ("a", 2, 2, 0), ("pair", 1, 0), ("a", 0, 3, 1), ("a", 0, 3, 0), ("zsum", 2), ("pair", 2, 0),
    ("b", 2, 0), ("pair", 2, 1), ("pair", 2, 7), ("pair", 0, 0), ("zsum", 6), ("b", 2, 1), ("zsum", 1),
    ("a", 1, 4, 1), ("zsum", 7), ("a", 1, 4, 0), ("a", 2, 3, 0), ("a", 2, 3, 1), ("a", 0, 4, 1), ("zsum", 0),
    ("a", 0, 4, 0), ("b", 3, 0), ("b", 3, 1), ("a", 2, 4, 0), ("a", 2, 4, 1), ("end",), ("b", 4, 0), ("b", 4, 1),
)
HITS_SENT, LOSS_DONE = 36, 78


def kernel(seqs, hidden_hbm, head_hbm, small, out, loss,
           hidden, head, in_sem,
           scores, peaks, grad, stats, hits,
           core_in, ya0, ya, za, yb0, yb, zb, last,
           lse_s, lse_r, hit_s, hit_r, core_s, core_r,
           ya_s, ya_r, za_s, za_r, yb_s, yb_r, zb_s, zb_r):
    vocab_rows, width = head.shape
    slots = hidden.shape[0]
    part = vocab_rows // NZ
    block = vocab_rows * width // LANES // (NZ * NY * NC)
    pitch = width // LANES
    rows_b = block - ROWS_A
    half_a, half_b = ROWS_A // 2, rows_b // 2

    depth = width // STEPS
    loads = []
    for i in range(STEPS):
        columns = pl.ds(i * depth, depth)
        loads.append((
            pltpu.make_async_copy(hidden_hbm.at[:, columns], hidden.at[:, columns], in_sem.at[0, i]),
            pltpu.make_async_copy(head_hbm.at[:, columns], head.at[:, columns], in_sem.at[1, i]),
        ))
        for load in loads[i]:
            load.start()

    v = lax.axis_index("vocab")
    d = lax.axis_index("dp")
    x = v % NX
    h = v // NX
    c = d % NC
    y = (d // NC) % NY
    z = d // (NC * NY)

    partner = d + 1 - 2 * c
    y_next = [(z * NY + (y + 1) % NY) * NC + c, (z * NY + (y + NY - 1) % NY) * NC + c]
    z_peer = [(((z + k) % NZ) * NY + y) * NC + c for k in (1, 2)]
    v_peers = [
        ((h + dh) % NH) * NX + (x + dx) % NX
        for dh in (2, 1, 3, 0) for dx in (2, 1, 3, 0) if dh or dx
    ]

    barrier = pltpu.get_barrier_semaphore()
    for peer in v_peers:
        pl.semaphore_signal(barrier, inc=1, device_id={"vocab": peer}, device_id_type=MESH)
    for peer in [partner] + y_next + z_peer:
        pl.semaphore_signal(barrier, inc=1, device_id={"dp": peer}, device_id_type=MESH)

    position = lax.broadcasted_iota(jnp.int32, (1, slots), 1)
    sizes = small[:, slots:slots + LANES]
    member, counts = [], []
    begin = jnp.zeros((1, 1), jnp.int32)
    weight = jnp.zeros((1, slots), F32)
    for k in range(seqs):
        count = sizes[:, k:k + 1]
        end = begin + count
        inside = (position >= begin) & (position < end)
        member.append(inside)
        counts.append(count.astype(F32))
        rate = sizes[:, seqs + k:seqs + k + 1].astype(F32) / counts[k]
        weight = jnp.where(inside, rate, weight)
        begin = end

    relative = small[:, 0:slots] - v * vocab_rows
    row = lax.broadcasted_iota(jnp.int32, (part, slots), 0)
    own_hit = jnp.zeros((1, slots), F32)
    part_lse = []
    for i in range(STEPS):
        for load in loads[i]:
            load.wait()
        columns = pl.ds(i * depth, depth)
        for k in range(NZ):
            value = lax.dot_general(
                head[pl.ds(k * part, part), columns], hidden[:, columns],
                (((1,), (1,)), ((), ())), preferred_element_type=F32,
            )
            if i > 0:
                value = value + scores[k]
            if i == STEPS - 1:
                peak = jnp.max(value, axis=0, keepdims=True)
                own_hit += jnp.sum(
                    jnp.where(row == relative - k * part, value, 0.0), axis=0, keepdims=True
                )
                value = jnp.exp(value - peak)
                peaks[k] = peak
                part_lse.append(peak + jnp.log(jnp.sum(value, axis=0, keepdims=True)))
            scores[k] = value

    def log_sum_exp(terms):
        top = terms[0]
        for term in terms[1:]:
            top = jnp.maximum(top, term)
        total = jnp.exp(terms[0] - top)
        for term in terms[1:]:
            total = total + jnp.exp(term - top)
        return top + jnp.log(total)

    stats[0] = log_sum_exp(part_lse)
    hits[0] = own_hit

    pl.semaphore_wait(barrier, NX * NH - 1 + 1 + 2 + 2)

    waits = []

    def send(src, dst, send_sem, recv_sem, axis, peer):
        copy = pltpu.make_async_remote_copy(
            src_ref=src, dst_ref=dst, send_sem=send_sem, recv_sem=recv_sem,
            device_id={axis: peer}, device_id_type=MESH,
        )
        copy.start()
        waits.append(copy)
        return copy

    def spread(ref, send_sem, recv_sem):
        return [
            send(ref.at[0], ref.at[s], send_sem.at[s], recv_sem.at[s], "vocab", peer)
            for s, peer in enumerate(v_peers, 1)
        ]

    def collect(copies, ref):
        for copy in copies:
            copy.wait_recv()
        return [ref[s] for s in range(NX * NH)]

    lse_copies = spread(stats, lse_s, lse_r)
    log_total = log_sum_exp(collect(lse_copies, stats))

    def line(zo, yo, co):
        return pl.multiple_of(((zo * NY + yo) * NC + co) * block, 8)

    def own(zo, yo, start, count):
        return pl.ds(pl.multiple_of(line(zo, yo, c) + start, 8), count)

    zone = [(z + 1) % NZ, (z + 2) % NZ, z]
    core_copies, ya_copies, za_copies, yb_copies, zb_copies = {}, {}, {}, {}, {}

    def product(k):
        zo = zone[k]
        onehot = jnp.where(row == relative - zo * part, 1.0, 0.0)
        shift = jnp.exp(peaks[zo] - log_total)
        rows = ((scores[zo] * shift - onehot) * weight).astype(jnp.bfloat16)
        value = jnp.dot(rows, hidden[...], preferred_element_type=F32)
        for j in range(pitch):
            grad[pl.ds(zo * part * pitch + j, part, stride=pitch), :] = value[:, j * LANES:(j + 1) * LANES]

    def swap(k, dist):
        i = DISTANCES.index(dist)
        core_copies[k, dist] = send(
            grad.at[pl.ds(line(zone[k], (y + dist) % NY, 1 - c), block)], core_in.at[k, i],
            core_s.at[k, i], core_r.at[k, i], "dp", partner,
        )

    def pair(k, dist):
        yo = (y + dist) % NY
        core_copies[k, dist].wait_recv()
        grad[own(zone[k], yo, 0, block), :] += core_in[k, DISTANCES.index(dist)]
        if dist == 4:
            for way in range(2):
                ya_copies[k, 0, way] = send(
                    grad.at[own(zone[k], yo, way * half_a, half_a)], ya0.at[k, way],
                    ya_s.at[k, 0, way], ya_r.at[k, 0, way], "dp", y_next[way],
                )
        if k < 2:
            zb_copies[k, dist] = send(
                grad.at[own(zone[k], yo, ROWS_A, rows_b)], zb.at[k, dist],
                zb_s.at[k, dist], zb_r.at[k, dist], "dp", z_peer[k],
            )

    def a(k, t, way):
        yo = (y + toward(way, t)) % NY
        ya_copies[k, t - 1, way].wait_recv()
        if t == 1:
            grad[own(zone[k], yo, way * half_a, half_a), :] += ya0[k, way]
        else:
            grad[own(zone[k], yo, 0, ROWS_A), :] += ya[k, t - 2, way]
        if t < 4:
            ya_copies[k, t, way] = send(
                grad.at[own(zone[k], yo, 0, ROWS_A)], ya.at[k, t - 1, way],
                ya_s.at[k, t, way], ya_r.at[k, t, way], "dp", y_next[way],
            )
            return
        closed.append((k, way))
        if k < 2 and (k, 1 - way) in closed:
            za_copies[k] = send(
                grad.at[own(zone[k], y, 0, ROWS_A)], za.at[k], za_s.at[k], za_r.at[k], "dp", z_peer[k]
            )

    closed = []

    def zsum(dist):
        yo = (y + dist) % NY
        for k in range(2):
            zb_copies[k, dist].wait_recv()
        grad[own(z, yo, ROWS_A, rows_b), :] += zb[0, dist] + zb[1, dist]
        if dist == 4:
            for way in range(2):
                yb_copies[0, way] = send(
                    grad.at[own(z, yo, ROWS_A + way * half_b, half_b)], yb0.at[way],
                    yb_s.at[0, way], yb_r.at[0, way], "dp", y_next[way],
                )

    def b(t, way):
        yo = (y + toward(way, t)) % NY
        yb_copies[t - 1, way].wait_recv()
        if t == 1:
            grad[own(z, yo, ROWS_A + way * half_b, half_b), :] += yb0[way]
        else:
            grad[own(z, yo, ROWS_A, rows_b), :] += yb[t - 2, way]
        if t < 4:
            yb_copies[t, way] = send(
                grad.at[own(z, yo, ROWS_A, rows_b)], yb.at[t - 1, way],
                yb_s.at[t, way], yb_r.at[t, way], "dp", y_next[way],
            )

    def end():
        for k in range(2):
            za_copies[k].wait_recv()
        last[pl.ds(0, ROWS_A), :] = grad[own(z, y, 0, ROWS_A), :] + za[0] + za[1]

    def finish_loss():
        target_logit = jnp.zeros((1, slots), F32)
        for term in collect(hit_copies, hits):
            target_logit = target_logit + term
        cross = log_total - target_logit
        for k in range(seqs):
            mean = jnp.where(member[k], cross, 0.0) / counts[k]
            loss[k] = jnp.sum(mean)

    steps = {"product": product, "swap": swap, "pair": pair, "a": a, "zsum": zsum, "b": b, "end": end}
    for number, (kind, *where) in enumerate(ORDER):
        if number == HITS_SENT:
            hit_copies = spread(hits, hit_s, hit_r)
        if number == LOSS_DONE:
            finish_loss()
        steps[kind](*where)

    last[pl.ds(ROWS_A, rows_b), :] = grad[own(z, y, ROWS_A, rows_b), :]
    for j in range(pitch):
        out[:, j * LANES:(j + 1) * LANES] = last[pl.ds(j, out.shape[0], stride=pitch), :]

    for copy in waits:
        copy.wait_send()


def on_device(hidden, head, targets, mask_counts, answer_lengths):
    vocab_rows, width = head.shape
    slots = hidden.shape[0]
    lines = vocab_rows * width // LANES
    block = lines // (NZ * NY * NC)
    rows_b = block - ROWS_A
    anywhere = pl.BlockSpec(memory_space=pl.ANY)
    vmem = pl.BlockSpec(memory_space=pltpu.VMEM)
    smem = pl.BlockSpec(memory_space=pltpu.SMEM)
    dma = pltpu.SemaphoreType.DMA
    seqs = mask_counts.shape[0]
    small = jnp.concatenate(
        [targets, mask_counts, answer_lengths, jnp.zeros((LANES - 2 * seqs,), jnp.int32)]
    ).reshape(1, slots + LANES)
    head_grad, seq_loss = pl.pallas_call(
        functools.partial(kernel, seqs),
        out_shape=(
            jax.ShapeDtypeStruct((vocab_rows // (NZ * NY * NC), width), F32),
            jax.ShapeDtypeStruct(mask_counts.shape, F32),
        ),
        in_specs=[anywhere, anywhere, vmem],
        out_specs=(vmem, smem),
        scratch_shapes=[
            pltpu.VMEM(hidden.shape, hidden.dtype),
            pltpu.VMEM(head.shape, head.dtype),
            dma((2, STEPS)),
            pltpu.VMEM((NZ, vocab_rows // NZ, slots), F32),
            pltpu.VMEM((NZ, 1, slots), F32),
            pltpu.VMEM((lines, LANES), F32),
            pltpu.VMEM((NX * NH, 1, slots), F32),
            pltpu.VMEM((NX * NH, 1, slots), F32),
            pltpu.VMEM((NZ, NY, block, LANES), F32),
            pltpu.VMEM((NZ, 2, ROWS_A // 2, LANES), F32),
            pltpu.VMEM((NZ, 3, 2, ROWS_A, LANES), F32),
            pltpu.VMEM((2, ROWS_A, LANES), F32),
            pltpu.VMEM((2, rows_b // 2, LANES), F32),
            pltpu.VMEM((3, 2, rows_b, LANES), F32),
            pltpu.VMEM((2, NY, rows_b, LANES), F32),
            pltpu.VMEM((block, LANES), F32),
            dma((NX * NH,)), dma((NX * NH,)),
            dma((NX * NH,)), dma((NX * NH,)),
            dma((NZ, NY)), dma((NZ, NY)),
            dma((NZ, 4, 2)), dma((NZ, 4, 2)),
            dma((2,)), dma((2,)),
            dma((4, 2)), dma((4, 2)),
            dma((2, NY)), dma((2, NY)),
        ],
        compiler_params=pltpu.CompilerParams(
            collective_id=0, has_side_effects=True, vmem_limit_bytes=52 * 1024 * 1024
        ),
        cost_estimate=pl.CostEstimate(
            flops=4 * vocab_rows * slots * width,
            bytes_accessed=2 * (vocab_rows + slots) * width,
            transcendentals=vocab_rows * slots,
        ),
        name="head_gradient",
    )(hidden, head, small)
    return seq_loss, head_grad


def solution(mesh):
    return jax.shard_map(
        on_device,
        mesh=mesh,
        in_specs=(P("dp", None), P("vocab", None), P("dp"), P("dp"), P("dp")),
        out_specs=(P("dp"), P(("vocab", "dp"), None)),
        check_vma=False,
    )
```

time: 373 us -> 62.1 us (0.17)
  the two profiles are of different devices: /device:TPU:562 before, /device:TPU:1 now
where the time goes in v2:
time: 62.1 us; the launch traced here: 61.9 us
  Pallas kernels  59.3 us (95%)
  local copies, waits for them, and re-layouts  1.2 us (2%)
  other arithmetic  0.8 us (1%)
  between operations  0.65 us (1%)
    pallas_call x1, Pallas kernels, on_device(): pl.pallas_call(functools.partial(kernel, seqs), out_shape=(jax.ShapeDtype...  59.3 us

profile of v2, /device:TPU:1, one launch (start us, length us, event | category | flops | bytes accessed | tf_op | source)
XLA Modules:
  0.0 61.9 jit_solution(8950643484956729149)
XLA Ops:
  0.6 0.8 %pad_add_fusion = s32[768]{0:T(1024)S(1)} fusion(s32[120]{0:T(128)S(1)} %broadcast_in_dim.3, s32[4]{0:T(128)} %param.9, s32[4]{0:T(128)} %param.8, s32[640]{0:T(1024)} %param.7), kind=kLoop, calls=%fused_computation | loop fusion | flops 2304 | bytes 6144 | tf_op jit(solution)/shard_map/concatenate | solution.py:297
  1.4 59.3 %head_gradient.1 = (f32[18,2048]{1,0:T(8,128)S(1)}, f32[4]{0:T(128)S(1)}) custom-call(bf16[640,2048]{1,0:T(8,128)(2,1)} %hidden_hbm.1, bf16[864,2048]{1,0:T(8,128)(2,1)} %head_hbm.1, s32[1,768]{1,0:T(1,128)S(1)} %reshape.7.small), custom_call_target="tpu_custom_call" | custom-call | flops 4529848320 | bytes 6160384 | tf_op jit(solution)/shard_map/head_gradient/pallas_call | solution.py:300
  60.7 0.5 copy.9
  61.2 0.7 %copy.10 = f32[18,2048]{1,0:T(8,128)} copy(f32[18,2048]{1,0:T(8,128)S(1)} %get-tuple-element.9) | data formatting | bytes 294912
  (2 shorter events, 0.0 us)

commit v3 on v2

--- a/solution.py
+++ b/solution.py
@@ -15,6 +15,7 @@
 LANES = 128
 STEPS = 4
 ROWS_A = 176
+HALVES_A, HALVES_B = (88, 88), (56, 56)
 DISTANCES = (4, 3, 5, 2, 6, 1, 7, 0)
 
 
@@ -23,26 +24,27 @@
 
 
 ORDER = (
-    ("product", 1), ("swap", 1, 4), ("product", 0), ("pair", 1, 4), ("swap", 0, 4), ("product", 2), ("swap", 2, 4),
-    ("swap", 1, 5), ("pair", 0, 4), ("swap", 1, 3), ("swap", 1, 0), ("pair", 2, 4), ("pair", 1, 5), ("swap", 0, 5),
-    ("swap", 0, 3), ("swap", 0, 6), ("swap", 0, 1), ("pair", 1, 3), ("a", 1, 1, 0), ("a", 1, 1, 1), ("swap", 2, 5),
-    ("swap", 1, 7), ("swap", 2, 2), ("pair", 0, 3), ("a", 0, 1, 0), ("swap", 2, 6), ("swap", 1, 6), ("pair", 0, 5),
-    ("swap", 2, 3), ("swap", 1, 1), ("a", 0, 1, 1), ("swap", 0, 7), ("zsum", 4), ("swap", 1, 2), ("pair", 2, 3),
-    ("pair", 1, 1), ("pair", 0, 6), ("pair", 1, 6), ("pair", 1, 7), ("pair", 2, 5), ("a", 2, 1, 0), ("a", 2, 1, 1),
-    ("swap", 2, 7), ("pair", 1, 2), ("a", 1, 2, 0), ("a", 1, 2, 1), ("pair", 0, 1), ("swap", 0, 0), ("pair", 2, 6),
-    ("swap", 2, 1), ("zsum", 3), ("swap", 0, 2), ("pair", 0, 2), ("b", 1, 0), ("zsum", 5), ("pair", 0, 7),
-    ("a", 0, 2, 1), ("b", 1, 1), ("a", 0, 2, 0), ("a", 2, 2, 1), ("a", 1, 3, 0), ("a", 1, 3, 1), ("pair", 2, 2),
-    ("swap", 2, 0), ("a", 2, 2, 0), ("pair", 1, 0), ("a", 0, 3, 1), ("a", 0, 3, 0), ("zsum", 2), ("pair", 2, 0),
-    ("b", 2, 0), ("pair", 2, 1), ("pair", 2, 7), ("pair", 0, 0), ("zsum", 6), ("b", 2, 1), ("zsum", 1),
-    ("a", 1, 4, 1), ("zsum", 7), ("a", 1, 4, 0), ("a", 2, 3, 0), ("a", 2, 3, 1), ("a", 0, 4, 1), ("zsum", 0),
-    ("a", 0, 4, 0), ("b", 3, 0), ("b", 3, 1), ("a", 2, 4, 0), ("a", 2, 4, 1), ("end",), ("b", 4, 0), ("b", 4, 1),
+    ("product", 1, 0), ("swap", 1, 4), ("product", 0, 0), ("swap", 0, 4), ("pair", 1, 4), ("product", 2, 0),
+    ("swap", 2, 4), ("pair", 0, 4), ("product", 1, 1), ("swap", 1, 3), ("swap", 1, 5), ("pair", 2, 4),
+    ("product", 0, 1), ("swap", 0, 7), ("swap", 0, 3), ("pair", 1, 3), ("swap", 0, 5), ("swap", 1, 6), ("pair", 1, 5),
+    ("a", 1, 1, 0), ("a", 1, 1, 1), ("product", 2, 1), ("pair", 0, 3), ("swap", 1, 2), ("zsum", 4), ("a", 0, 1, 0),
+    ("pair", 1, 6), ("swap", 0, 0), ("pair", 0, 5), ("a", 0, 1, 1), ("swap", 2, 3), ("swap", 2, 5), ("swap", 2, 0),
+    ("swap", 0, 2), ("swap", 2, 6), ("pair", 2, 3), ("pair", 1, 2), ("pair", 2, 5), ("swap", 0, 6), ("swap", 1, 7),
+    ("a", 2, 1, 0), ("a", 2, 1, 1), ("pair", 0, 2), ("swap", 2, 2), ("swap", 1, 1), ("pair", 0, 6), ("a", 1, 2, 0),
+    ("pair", 2, 2), ("a", 1, 2, 1), ("swap", 1, 0), ("pair", 2, 6), ("pair", 1, 7), ("a", 0, 2, 0), ("swap", 2, 1),
+    ("a", 0, 2, 1), ("a", 2, 2, 1), ("zsum", 3), ("pair", 0, 0), ("b", 1, 0), ("swap", 0, 1), ("zsum", 2),
+    ("zsum", 5), ("pair", 1, 0), ("pair", 1, 1), ("a", 1, 3, 0), ("b", 1, 1), ("pair", 0, 1), ("a", 2, 2, 0),
+    ("a", 1, 3, 1), ("pair", 0, 7), ("zsum", 6), ("a", 0, 3, 1), ("swap", 2, 7), ("a", 0, 3, 0), ("pair", 2, 1),
+    ("hits",), ("pair", 2, 7), ("b", 2, 0), ("pair", 2, 0), ("b", 2, 1), ("a", 2, 3, 1), ("a", 2, 3, 0),
+    ("a", 1, 4, 1), ("a", 1, 4, 0), ("zsum", 7), ("a", 0, 4, 0), ("zsum", 1), ("zsum", 0), ("a", 0, 4, 1),
+    ("b", 3, 0), ("b", 3, 1), ("a", 2, 4, 0), ("loss",), ("a", 2, 4, 1), ("sent",), ("end",), ("b", 4, 0),
+    ("b", 4, 1),
 )
-HITS_SENT, LOSS_DONE = 36, 78
 
 
 def kernel(seqs, hidden_hbm, head_hbm, small, out, loss,
            hidden, head, in_sem,
-           scores, peaks, grad, stats, hits,
+           scores, marks, peaks, grad, stats, hits,
            core_in, ya0, ya, za, yb0, yb, zb, last,
            lse_s, lse_r, hit_s, hit_r, core_s, core_r,
            ya_s, ya_r, za_s, za_r, yb_s, yb_r, zb_s, zb_r):
@@ -52,7 +54,7 @@
     block = vocab_rows * width // LANES // (NZ * NY * NC)
     pitch = width // LANES
     rows_b = block - ROWS_A
-    half_a, half_b = ROWS_A // 2, rows_b // 2
+    from_a, from_b = (0, HALVES_A[0]), (ROWS_A, ROWS_A + HALVES_B[0])
 
     depth = width // STEPS
     loads = []
@@ -104,7 +106,6 @@
 
     relative = small[:, 0:slots] - v * vocab_rows
     row = lax.broadcasted_iota(jnp.int32, (part, slots), 0)
-    own_hit = jnp.zeros((1, slots), F32)
     part_lse = []
     for i in range(STEPS):
         for load in loads[i]:
@@ -119,9 +120,7 @@
                 value = value + scores[k]
             if i == STEPS - 1:
                 peak = jnp.max(value, axis=0, keepdims=True)
-                own_hit += jnp.sum(
-                    jnp.where(row == relative - k * part, value, 0.0), axis=0, keepdims=True
-                )
+                marks[k] = value
                 value = jnp.exp(value - peak)
                 peaks[k] = peak
                 part_lse.append(peak + jnp.log(jnp.sum(value, axis=0, keepdims=True)))
@@ -137,7 +136,6 @@
         return top + jnp.log(total)
 
     stats[0] = log_sum_exp(part_lse)
-    hits[0] = own_hit
 
     pl.semaphore_wait(barrier, NX * NH - 1 + 1 + 2 + 2)
 
@@ -164,6 +162,14 @@
         return [ref[s] for s in range(NX * NH)]
 
     lse_copies = spread(stats, lse_s, lse_r)
+
+    own_hit = jnp.zeros((1, slots), F32)
+    for k in range(NZ):
+        hit = row == relative - k * part
+        own_hit += jnp.sum(jnp.where(hit, marks[k], 0.0), axis=0, keepdims=True)
+        marks[k] = jnp.where(hit, weight, 0.0)
+    hits[0] = own_hit
+
     log_total = log_sum_exp(collect(lse_copies, stats))
 
     def line(zo, yo, co):
@@ -175,14 +181,17 @@
     zone = [(z + 1) % NZ, (z + 2) % NZ, z]
     core_copies, ya_copies, za_copies, yb_copies, zb_copies = {}, {}, {}, {}, {}
 
-    def product(k):
+    def product(k, second):
         zo = zone[k]
-        onehot = jnp.where(row == relative - zo * part, 1.0, 0.0)
-        shift = jnp.exp(peaks[zo] - log_total)
-        rows = ((scores[zo] * shift - onehot) * weight).astype(jnp.bfloat16)
-        value = jnp.dot(rows, hidden[...], preferred_element_type=F32)
+        half = part // 2
+        start = pl.multiple_of((((y + 4) % NY) // 4 + second) % 2 * half, 8)
+        rows = pl.ds(start, half)
+        scale = jnp.exp(peaks[zo] - log_total) * weight
+        value = (scores[zo, rows, :] * scale - marks[zo, rows, :]).astype(jnp.bfloat16)
+        value = jnp.dot(value, hidden[...], preferred_element_type=F32)
+        first = (zo * part + start) * pitch
         for j in range(pitch):
-            grad[pl.ds(zo * part * pitch + j, part, stride=pitch), :] = value[:, j * LANES:(j + 1) * LANES]
+            grad[pl.ds(first + j, half, stride=pitch), :] = value[:, j * LANES:(j + 1) * LANES]
 
     def swap(k, dist):
         i = DISTANCES.index(dist)
@@ -198,7 +207,8 @@
         if dist == 4:
             for way in range(2):
                 ya_copies[k, 0, way] = send(
-                    grad.at[own(zone[k], yo, way * half_a, half_a)], ya0.at[k, way],
+                    grad.at[own(zone[k], yo, from_a[way], HALVES_A[way])],
+                    ya0.at[k, way, pl.ds(0, HALVES_A[way])],
                     ya_s.at[k, 0, way], ya_r.at[k, 0, way], "dp", y_next[way],
                 )
         if k < 2:
@@ -211,7 +221,7 @@
         yo = (y + toward(way, t)) % NY
         ya_copies[k, t - 1, way].wait_recv()
         if t == 1:
-            grad[own(zone[k], yo, way * half_a, half_a), :] += ya0[k, way]
+            grad[own(zone[k], yo, from_a[way], HALVES_A[way]), :] += ya0[k, way, pl.ds(0, HALVES_A[way]), :]
         else:
             grad[own(zone[k], yo, 0, ROWS_A), :] += ya[k, t - 2, way]
         if t < 4:
@@ -236,7 +246,8 @@
         if dist == 4:
             for way in range(2):
                 yb_copies[0, way] = send(
-                    grad.at[own(z, yo, ROWS_A + way * half_b, half_b)], yb0.at[way],
+                    grad.at[own(z, yo, from_b[way], HALVES_B[way])],
+                    yb0.at[way, pl.ds(0, HALVES_B[way])],
                     yb_s.at[0, way], yb_r.at[0, way], "dp", y_next[way],
                 )
 
@@ -244,7 +255,7 @@
         yo = (y + toward(way, t)) % NY
         yb_copies[t - 1, way].wait_recv()
         if t == 1:
-            grad[own(z, yo, ROWS_A + way * half_b, half_b), :] += yb0[way]
+            grad[own(z, yo, from_b[way], HALVES_B[way]), :] += yb0[way, pl.ds(0, HALVES_B[way]), :]
         else:
             grad[own(z, yo, ROWS_A, rows_b), :] += yb[t - 2, way]
         if t < 4:
@@ -257,6 +268,11 @@
         for k in range(2):
             za_copies[k].wait_recv()
         last[pl.ds(0, ROWS_A), :] = grad[own(z, y, 0, ROWS_A), :] + za[0] + za[1]
+
+    hit_copies = []
+
+    def send_hits():
+        hit_copies.extend(spread(hits, hit_s, hit_r))
 
     def finish_loss():
         target_logit = jnp.zeros((1, slots), F32)
@@ -267,12 +283,14 @@
             mean = jnp.where(member[k], cross, 0.0) / counts[k]
             loss[k] = jnp.sum(mean)
 
-    steps = {"product": product, "swap": swap, "pair": pair, "a": a, "zsum": zsum, "b": b, "end": end}
-    for number, (kind, *where) in enumerate(ORDER):
-        if number == HITS_SENT:
-            hit_copies = spread(hits, hit_s, hit_r)
-        if number == LOSS_DONE:
-            finish_loss()
+    def sent():
+        for copy in waits[:-16]:
+            copy.wait_send()
+        del waits[:-16]
+
+    steps = {"product": product, "swap": swap, "pair": pair, "a": a, "zsum": zsum, "b": b, "end": end,
+             "hits": send_hits, "loss": finish_loss, "sent": sent}
+    for kind, *where in ORDER:
         steps[kind](*where)
 
     last[pl.ds(ROWS_A, rows_b), :] = grad[own(z, y, ROWS_A, rows_b), :]
@@ -310,15 +328,16 @@
             pltpu.VMEM(head.shape, head.dtype),
             dma((2, STEPS)),
             pltpu.VMEM((NZ, vocab_rows // NZ, slots), F32),
+            pltpu.VMEM((NZ, vocab_rows // NZ, slots), F32),
             pltpu.VMEM((NZ, 1, slots), F32),
             pltpu.VMEM((lines, LANES), F32),
             pltpu.VMEM((NX * NH, 1, slots), F32),
             pltpu.VMEM((NX * NH, 1, slots), F32),
             pltpu.VMEM((NZ, NY, block, LANES), F32),
-            pltpu.VMEM((NZ, 2, ROWS_A // 2, LANES), F32),
+            pltpu.VMEM((NZ, 2, max(HALVES_A), LANES), F32),
             pltpu.VMEM((NZ, 3, 2, ROWS_A, LANES), F32),
             pltpu.VMEM((2, ROWS_A, LANES), F32),
-            pltpu.VMEM((2, rows_b // 2, LANES), F32),
+            pltpu.VMEM((2, max(HALVES_B), LANES), F32),
             pltpu.VMEM((3, 2, rows_b, LANES), F32),
             pltpu.VMEM((2, NY, rows_b, LANES), F32),
             pltpu.VMEM((block, LANES), F32),

time: 62.1 us -> 61.2 us (0.986)
  Pallas kernels: 59.3 us -> 58.2 us
    pallas_call x1, Pallas kernels: 59.3 us -> 58.2 us  [on_device(): pl.pallas_call(functools.partial(kernel, seqs), out_shape=(jax.ShapeDtype...]
where the time goes in v3:
time: 61.2 us; the launch traced here: 60.8 us
  Pallas kernels  58.2 us (95%)
  local copies, waits for them, and re-layouts  1.2 us (2%)
  other arithmetic  0.8 us (1%)
  between operations  0.65 us (1%)
    pallas_call x1, Pallas kernels, on_device(): pl.pallas_call(functools.partial(kernel, seqs), out_shape=(jax.ShapeDtype...  58.2 us

profile of v3, /device:TPU:1, one launch (start us, length us, event | category | flops | bytes accessed | tf_op | source)
XLA Modules:
  0.0 60.8 jit_solution(12114591308133445703)
XLA Ops:
  0.6 0.8 %pad_add_fusion = s32[768]{0:T(1024)S(1)} fusion(s32[120]{0:T(128)S(1)} %broadcast_in_dim.3, s32[4]{0:T(128)} %param.9, s32[4]{0:T(128)} %param.8, s32[640]{0:T(1024)} %param.7), kind=kLoop, calls=%fused_computation | loop fusion | flops 2304 | bytes 6144 | tf_op jit(solution)/shard_map/concatenate | solution.py:315
  1.4 58.2 %head_gradient.1 = (f32[18,2048]{1,0:T(8,128)S(1)}, f32[4]{0:T(128)S(1)}) custom-call(bf16[640,2048]{1,0:T(8,128)(2,1)} %hidden_hbm.1, bf16[864,2048]{1,0:T(8,128)(2,1)} %head_hbm.1, s32[1,768]{1,0:T(1,128)S(1)} %reshape.7.small), custom_call_target="tpu_custom_call" | custom-call | flops 4529848320 | bytes 6160384 | tf_op jit(solution)/shard_map/head_gradient/pallas_call | solution.py:318
  59.6 0.5 copy.9
  60.2 0.7 %copy.10 = f32[18,2048]{1,0:T(8,128)} copy(f32[18,2048]{1,0:T(8,128)S(1)} %get-tuple-element.9) | data formatting | bytes 294912
  (2 shorter events, 0.0 us)

commit v4 on v3

--- a/solution.py
+++ b/solution.py
@@ -1,5 +1,3 @@
-import functools
-
 import jax
 import jax.numpy as jnp
 from jax import lax
@@ -42,8 +40,8 @@
 )
 
 
-def kernel(seqs, hidden_hbm, head_hbm, small, out, loss,
-           hidden, head, in_sem,
+def kernel(hidden_hbm, head_hbm, targets_hbm, counts_hbm, lengths_hbm, out, loss,
+           hidden, head, targets, counts, lengths, in_sem, small_sem,
            scores, marks, peaks, grad, stats, hits,
            core_in, ya0, ya, za, yb0, yb, zb, last,
            lse_s, lse_r, hit_s, hit_r, core_s, core_r,
@@ -56,6 +54,26 @@
     rows_b = block - ROWS_A
     from_a, from_b = (0, HALVES_A[0]), (ROWS_A, ROWS_A + HALVES_B[0])
 
+    v = lax.axis_index("vocab")
+    d = lax.axis_index("dp")
+    x = v % NX
+    h = v // NX
+    c = d % NC
+    y = (d // NC) % NY
+    z = d // (NC * NY)
+
+    partner = d + 1 - 2 * c
+    y_next = [(z * NY + (y + 1) % NY) * NC + c, (z * NY + (y + NY - 1) % NY) * NC + c]
+    z_peer = [(((z + k) % NZ) * NY + y) * NC + c for k in (1, 2)]
+    v_peers = [
+        ((h + dh) % NH) * NX + (x + dx) % NX
+        for dh in (2, 1, 3, 0) for dx in (2, 1, 3, 0) if dh or dx
+    ]
+
+    barrier = pltpu.get_barrier_semaphore()
+    for peer in v_peers:
+        pl.semaphore_signal(barrier, inc=1, device_id={"vocab": peer}, device_id_type=MESH)
+    seqs = counts.shape[0]
     depth = width // STEPS
     loads = []
     for i in range(STEPS):
@@ -66,45 +84,16 @@
         ))
         for load in loads[i]:
             load.start()
-
-    v = lax.axis_index("vocab")
-    d = lax.axis_index("dp")
-    x = v % NX
-    h = v // NX
-    c = d % NC
-    y = (d // NC) % NY
-    z = d // (NC * NY)
-
-    partner = d + 1 - 2 * c
-    y_next = [(z * NY + (y + 1) % NY) * NC + c, (z * NY + (y + NY - 1) % NY) * NC + c]
-    z_peer = [(((z + k) % NZ) * NY + y) * NC + c for k in (1, 2)]
-    v_peers = [
-        ((h + dh) % NH) * NX + (x + dx) % NX
-        for dh in (2, 1, 3, 0) for dx in (2, 1, 3, 0) if dh or dx
+    small_loads = [
+        pltpu.make_async_copy(targets_hbm, targets, small_sem.at[0]),
+        pltpu.make_async_copy(counts_hbm, counts, small_sem.at[1]),
+        pltpu.make_async_copy(lengths_hbm, lengths, small_sem.at[2]),
     ]
-
-    barrier = pltpu.get_barrier_semaphore()
-    for peer in v_peers:
-        pl.semaphore_signal(barrier, inc=1, device_id={"vocab": peer}, device_id_type=MESH)
+    for load in small_loads:
+        load.start()
     for peer in [partner] + y_next + z_peer:
         pl.semaphore_signal(barrier, inc=1, device_id={"dp": peer}, device_id_type=MESH)
 
-    position = lax.broadcasted_iota(jnp.int32, (1, slots), 1)
-    sizes = small[:, slots:slots + LANES]
-    member, counts = [], []
-    begin = jnp.zeros((1, 1), jnp.int32)
-    weight = jnp.zeros((1, slots), F32)
-    for k in range(seqs):
-        count = sizes[:, k:k + 1]
-        end = begin + count
-        inside = (position >= begin) & (position < end)
-        member.append(inside)
-        counts.append(count.astype(F32))
-        rate = sizes[:, seqs + k:seqs + k + 1].astype(F32) / counts[k]
-        weight = jnp.where(inside, rate, weight)
-        begin = end
-
-    relative = small[:, 0:slots] - v * vocab_rows
     row = lax.broadcasted_iota(jnp.int32, (part, slots), 0)
     part_lse = []
     for i in range(STEPS):
@@ -163,6 +152,22 @@
 
     lse_copies = spread(stats, lse_s, lse_r)
 
+    for load in small_loads:
+        load.wait()
+    position = lax.broadcasted_iota(jnp.int32, (1, slots), 1)
+    member, sizes = [], []
+    begin = jnp.int32(0)
+    weight = jnp.zeros((1, slots), F32)
+    for k in range(seqs):
+        end_of = begin + counts[k]
+        inside = (position >= begin) & (position < end_of)
+        member.append(inside)
+        sizes.append(jnp.full((1, slots), counts[k], jnp.int32).astype(F32))
+        rate = jnp.full((1, slots), lengths[k], jnp.int32).astype(F32) / sizes[k]
+        weight = jnp.where(inside, rate, weight)
+        begin = end_of
+
+    relative = targets[...].reshape(1, slots) - v * vocab_rows
     own_hit = jnp.zeros((1, slots), F32)
     for k in range(NZ):
         hit = row == relative - k * part
@@ -280,7 +285,7 @@
             target_logit = target_logit + term
         cross = log_total - target_logit
         for k in range(seqs):
-            mean = jnp.where(member[k], cross, 0.0) / counts[k]
+            mean = jnp.where(member[k], cross, 0.0) / sizes[k]
             loss[k] = jnp.sum(mean)
 
     def sent():
@@ -307,26 +312,29 @@
     lines = vocab_rows * width // LANES
     block = lines // (NZ * NY * NC)
     rows_b = block - ROWS_A
-    anywhere = pl.BlockSpec(memory_space=pl.ANY)
+    anywhere = pl.BlockSpec(memory_space=pltpu.HBM)
     vmem = pl.BlockSpec(memory_space=pltpu.VMEM)
     smem = pl.BlockSpec(memory_space=pltpu.SMEM)
     dma = pltpu.SemaphoreType.DMA
-    seqs = mask_counts.shape[0]
-    small = jnp.concatenate(
-        [targets, mask_counts, answer_lengths, jnp.zeros((LANES - 2 * seqs,), jnp.int32)]
-    ).reshape(1, slots + LANES)
+    arguments = [
+        pltpu.with_memory_space_constraint(argument, pltpu.HBM)
+        for argument in (hidden, head, targets, mask_counts, answer_lengths)
+    ]
     head_grad, seq_loss = pl.pallas_call(
-        functools.partial(kernel, seqs),
+        kernel,
         out_shape=(
             jax.ShapeDtypeStruct((vocab_rows // (NZ * NY * NC), width), F32),
             jax.ShapeDtypeStruct(mask_counts.shape, F32),
         ),
-        in_specs=[anywhere, anywhere, vmem],
+        in_specs=[anywhere] * 5,
         out_specs=(vmem, smem),
         scratch_shapes=[
             pltpu.VMEM(hidden.shape, hidden.dtype),
             pltpu.VMEM(head.shape, head.dtype),
-            dma((2, STEPS)),
+            pltpu.VMEM(targets.shape, targets.dtype),
+            pltpu.SMEM(mask_counts.shape, mask_counts.dtype),
+            pltpu.SMEM(answer_lengths.shape, answer_lengths.dtype),
+            dma((2, STEPS)), dma((3,)),
             pltpu.VMEM((NZ, vocab_rows // NZ, slots), F32),
             pltpu.VMEM((NZ, vocab_rows // NZ, slots), F32),
             pltpu.VMEM((NZ, 1, slots), F32),
@@ -358,7 +366,7 @@
             transcendentals=vocab_rows * slots,
         ),
         name="head_gradient",
-    )(hidden, head, small)
+    )(*arguments)
     return seq_loss, head_grad
 
 

time: 61.2 us -> 60.6 us (level)
  other arithmetic: 0.8 us -> 0 us
    concatenate x1 -> x0, other arithmetic: 0.8 us -> none  [on_device(): jnp.concatenate([targets, mask_counts, answer_lengths, jnp.zeros((LANES -...]
where the time goes in v4:
time: 60.6 us; the launch traced here: 60.2 us
  Pallas kernels  58.4 us (96%)
  local copies, waits for them, and re-layouts  1.19 us (2%)
  between operations  0.64 us (1%)
    pallas_call x1, Pallas kernels, on_device(): pl.pallas_call(kernel, out_shape=(jax.ShapeDtypeStruct((vocab_rows // (NZ...  58.4 us

profile of v4, /device:TPU:1, one launch (start us, length us, event | category | flops | bytes accessed | tf_op | source)
XLA Modules:
  0.0 60.2 jit_solution(11756435126474222761)
XLA Ops:
  0.6 58.4 %head_gradient.1 = (f32[18,2048]{1,0:T(8,128)S(1)}, f32[4]{0:T(128)S(1)}) custom-call(bf16[640,2048]{1,0:T(8,128)(2,1)} %hidden_hbm.1, bf16[864,2048]{1,0:T(8,128)(2,1)} %head_hbm.1, s32[640]{0:T(1024)} %targets_hbm.1, s32[4]{0:T(128)} %counts_hbm.1, s32[4]{0:T(128)} %lengths_hbm.1), custom_call_target="tpu_custom_call" | custom-call | flops 4529848320 | bytes 6160384 | tf_op jit(solution)/shard_map/head_gradient/pallas_call | solution.py:323
  59.0 0.5 copy.9
  59.5 0.7 %copy.10 = f32[18,2048]{1,0:T(8,128)} copy(f32[18,2048]{1,0:T(8,128)S(1)} %get-tuple-element.9) | data formatting | bytes 294912

commit v5 on v4

--- a/solution.py
+++ b/solution.py
@@ -12,8 +12,8 @@
 NZ, NY, NC = 3, 8, 2
 LANES = 128
 STEPS = 4
-ROWS_A = 176
-HALVES_A, HALVES_B = (88, 88), (56, 56)
+ROWS_A = 168
+HALVES_A, HALVES_B = (88, 80), (56, 64)
 DISTANCES = (4, 3, 5, 2, 6, 1, 7, 0)
 
 
@@ -22,21 +22,21 @@
 
 
 ORDER = (
-    ("product", 1, 0), ("swap", 1, 4), ("product", 0, 0), ("swap", 0, 4), ("pair", 1, 4), ("product", 2, 0),
-    ("swap", 2, 4), ("pair", 0, 4), ("product", 1, 1), ("swap", 1, 3), ("swap", 1, 5), ("pair", 2, 4),
-    ("product", 0, 1), ("swap", 0, 7), ("swap", 0, 3), ("pair", 1, 3), ("swap", 0, 5), ("swap", 1, 6), ("pair", 1, 5),
-    ("a", 1, 1, 0), ("a", 1, 1, 1), ("product", 2, 1), ("pair", 0, 3), ("swap", 1, 2), ("zsum", 4), ("a", 0, 1, 0),
-    ("pair", 1, 6), ("swap", 0, 0), ("pair", 0, 5), ("a", 0, 1, 1), ("swap", 2, 3), ("swap", 2, 5), ("swap", 2, 0),
-    ("swap", 0, 2), ("swap", 2, 6), ("pair", 2, 3), ("pair", 1, 2), ("pair", 2, 5), ("swap", 0, 6), ("swap", 1, 7),
-    ("a", 2, 1, 0), ("a", 2, 1, 1), ("pair", 0, 2), ("swap", 2, 2), ("swap", 1, 1), ("pair", 0, 6), ("a", 1, 2, 0),
-    ("pair", 2, 2), ("a", 1, 2, 1), ("swap", 1, 0), ("pair", 2, 6), ("pair", 1, 7), ("a", 0, 2, 0), ("swap", 2, 1),
-    ("a", 0, 2, 1), ("a", 2, 2, 1), ("zsum", 3), ("pair", 0, 0), ("b", 1, 0), ("swap", 0, 1), ("zsum", 2),
-    ("zsum", 5), ("pair", 1, 0), ("pair", 1, 1), ("a", 1, 3, 0), ("b", 1, 1), ("pair", 0, 1), ("a", 2, 2, 0),
-    ("a", 1, 3, 1), ("pair", 0, 7), ("zsum", 6), ("a", 0, 3, 1), ("swap", 2, 7), ("a", 0, 3, 0), ("pair", 2, 1),
-    ("hits",), ("pair", 2, 7), ("b", 2, 0), ("pair", 2, 0), ("b", 2, 1), ("a", 2, 3, 1), ("a", 2, 3, 0),
-    ("a", 1, 4, 1), ("a", 1, 4, 0), ("zsum", 7), ("a", 0, 4, 0), ("zsum", 1), ("zsum", 0), ("a", 0, 4, 1),
-    ("b", 3, 0), ("b", 3, 1), ("a", 2, 4, 0), ("loss",), ("a", 2, 4, 1), ("sent",), ("end",), ("b", 4, 0),
-    ("b", 4, 1),
+    ("product", 1, 0), ("swap", 1, 4), ("product", 1, 1), ("product", 0, 0), ("pair", 1, 4), ("swap", 0, 4),
+    ("swap", 1, 5), ("product", 2, 0), ("swap", 1, 6), ("hits_x",), ("swap", 2, 4), ("swap", 1, 3), ("pair", 0, 4),
+    ("pair", 1, 5), ("product", 0, 1), ("pair", 2, 4), ("swap", 1, 2), ("pair", 1, 3), ("swap", 0, 2), ("swap", 0, 3),
+    ("swap", 0, 5), ("product", 2, 1), ("a", 1, 1, 1), ("swap", 2, 3), ("a", 1, 1, 0), ("pair", 0, 3), ("swap", 0, 6),
+    ("swap", 2, 1), ("pair", 0, 5), ("pair", 2, 3), ("swap", 2, 5), ("a", 0, 1, 0), ("swap", 2, 2), ("a", 0, 1, 1),
+    ("swap", 1, 0), ("swap", 2, 6), ("zsum", 4), ("swap", 1, 1), ("a", 2, 1, 0), ("pair", 0, 6), ("pair", 2, 5),
+    ("swap", 1, 7), ("swap", 2, 7), ("a", 2, 1, 1), ("pair", 1, 2), ("pair", 2, 6), ("pair", 1, 6), ("zsum", 3),
+    ("swap", 0, 7), ("pair", 2, 7), ("a", 1, 2, 1), ("a", 1, 2, 0), ("pair", 0, 2), ("pair", 1, 0), ("zsum", 5),
+    ("a", 0, 2, 0), ("hits_z",), ("pair", 2, 2), ("swap", 0, 0), ("b", 1, 1), ("a", 0, 2, 1), ("b", 1, 0),
+    ("pair", 0, 7), ("pair", 2, 1), ("swap", 0, 1), ("swap", 2, 0), ("pair", 0, 1), ("pair", 1, 1), ("pair", 1, 7),
+    ("a", 2, 2, 0), ("a", 2, 2, 1), ("pair", 0, 0), ("a", 1, 3, 0), ("zsum", 6), ("zsum", 2), ("a", 0, 3, 0),
+    ("a", 1, 3, 1), ("a", 0, 3, 1), ("b", 2, 0), ("a", 2, 3, 0), ("b", 2, 1), ("loss",), ("a", 2, 3, 1),
+    ("a", 1, 4, 1), ("a", 1, 4, 0), ("a", 0, 4, 0), ("pair", 2, 0), ("zsum", 1), ("a", 0, 4, 1), ("zsum", 7),
+    ("b", 3, 1), ("b", 3, 0), ("a", 2, 4, 0), ("zsum", 0), ("a", 2, 4, 1), ("sent",), ("end",), ("b", 4, 1),
+    ("b", 4, 0),
 )
 
 
@@ -70,8 +70,11 @@
         for dh in (2, 1, 3, 0) for dx in (2, 1, 3, 0) if dh or dx
     ]
 
+    x_peers = [h * NX + (x + i) % NX for i in range(1, NX)]
+    h_peers = [((h + i) % NH) * NX + x for i in range(1, NH)]
+
     barrier = pltpu.get_barrier_semaphore()
-    for peer in v_peers:
+    for peer in v_peers[8:12] + v_peers[:8] + v_peers[12:]:
         pl.semaphore_signal(barrier, inc=1, device_id={"vocab": peer}, device_id_type=MESH)
     seqs = counts.shape[0]
     depth = width // STEPS
@@ -139,18 +142,18 @@
         waits.append(copy)
         return copy
 
-    def spread(ref, send_sem, recv_sem):
+    def spread(ref, send_sem, recv_sem, peers, first=0):
         return [
-            send(ref.at[0], ref.at[s], send_sem.at[s], recv_sem.at[s], "vocab", peer)
-            for s, peer in enumerate(v_peers, 1)
+            send(ref.at[first], ref.at[s], send_sem.at[s], recv_sem.at[s], "vocab", peer)
+            for s, peer in enumerate(peers, first + 1)
         ]
 
-    def collect(copies, ref):
+    def collect(copies, ref, first=0):
         for copy in copies:
             copy.wait_recv()
-        return [ref[s] for s in range(NX * NH)]
-
-    lse_copies = spread(stats, lse_s, lse_r)
+        return [ref[first + s] for s in range(len(copies) + 1)]
+
+    lse_copies = spread(stats, lse_s, lse_r, v_peers)
 
     for load in small_loads:
         load.wait()
@@ -276,13 +279,15 @@
 
     hit_copies = []
 
-    def send_hits():
-        hit_copies.extend(spread(hits, hit_s, hit_r))
+    def hits_x():
+        hit_copies.extend(spread(hits, hit_s, hit_r, x_peers))
+
+    def hits_z():
+        hits[NX] = sum(collect(hit_copies, hits))
+        hit_copies[:] = spread(hits, hit_s, hit_r, h_peers, NX)
 
     def finish_loss():
-        target_logit = jnp.zeros((1, slots), F32)
-        for term in collect(hit_copies, hits):
-            target_logit = target_logit + term
+        target_logit = sum(collect(hit_copies, hits, NX))
         cross = log_total - target_logit
         for k in range(seqs):
             mean = jnp.where(member[k], cross, 0.0) / sizes[k]
@@ -294,7 +299,7 @@
         del waits[:-16]
 
     steps = {"product": product, "swap": swap, "pair": pair, "a": a, "zsum": zsum, "b": b, "end": end,
-             "hits": send_hits, "loss": finish_loss, "sent": sent}
+             "hits_x": hits_x, "hits_z": hits_z, "loss": finish_loss, "sent": sent}
     for kind, *where in ORDER:
         steps[kind](*where)
 
@@ -340,7 +345,7 @@
             pltpu.VMEM((NZ, 1, slots), F32),
             pltpu.VMEM((lines, LANES), F32),
             pltpu.VMEM((NX * NH, 1, slots), F32),
-            pltpu.VMEM((NX * NH, 1, slots), F32),
+            pltpu.VMEM((NX + NH, 1, slots), F32),
             pltpu.VMEM((NZ, NY, block, LANES), F32),
             pltpu.VMEM((NZ, 2, max(HALVES_A), LANES), F32),
             pltpu.VMEM((NZ, 3, 2, ROWS_A, LANES), F32),
@@ -350,7 +355,7 @@
             pltpu.VMEM((2, NY, rows_b, LANES), F32),
             pltpu.VMEM((block, LANES), F32),
             dma((NX * NH,)), dma((NX * NH,)),
-            dma((NX * NH,)), dma((NX * NH,)),
+            dma((NX + NH,)), dma((NX + NH,)),
             dma((NZ, NY)), dma((NZ, NY)),
             dma((NZ, 4, 2)), dma((NZ, 4, 2)),
             dma((2,)), dma((2,)),

time: 60.6 us -> 60 us (0.990)
  no operation moved by 1% of the time
where the time goes in v5:
time: 60 us; the launch traced here: 59.7 us
  Pallas kernels  57.8 us (96%)
  local copies, waits for them, and re-layouts  1.19 us (2%)
  between operations  0.64 us (1%)
    pallas_call x1, Pallas kernels, on_device(): pl.pallas_call(kernel, out_shape=(jax.ShapeDtypeStruct((vocab_rows // (NZ...  57.8 us

profile of v5, /device:TPU:1, one launch (start us, length us, event | category | flops | bytes accessed | tf_op | source)
XLA Modules:
  0.0 59.7 jit_solution(6117091444122785365)
XLA Ops:
  0.6 57.8 %head_gradient.1 = (f32[18,2048]{1,0:T(8,128)S(1)}, f32[4]{0:T(128)S(1)}) custom-call(bf16[640,2048]{1,0:T(8,128)(2,1)} %hidden_hbm.1, bf16[864,2048]{1,0:T(8,128)(2,1)} %head_hbm.1, s32[640]{0:T(1024)} %targets_hbm.1, s32[4]{0:T(128)} %counts_hbm.1, s32[4]{0:T(128)} %lengths_hbm.1), custom_call_target="tpu_custom_call" | custom-call | flops 4529848320 | bytes 6160384 | tf_op jit(solution)/shard_map/head_gradient/pallas_call | solution.py:328
  58.5 0.5 copy.9
  59.0 0.7 %copy.10 = f32[18,2048]{1,0:T(8,128)} copy(f32[18,2048]{1,0:T(8,128)S(1)} %get-tuple-element.9) | data formatting | bytes 294912

commit v6 on v5

--- a/solution.py
+++ b/solution.py
@@ -35,8 +35,8 @@
     ("a", 2, 2, 0), ("a", 2, 2, 1), ("pair", 0, 0), ("a", 1, 3, 0), ("zsum", 6), ("zsum", 2), ("a", 0, 3, 0),
     ("a", 1, 3, 1), ("a", 0, 3, 1), ("b", 2, 0), ("a", 2, 3, 0), ("b", 2, 1), ("loss",), ("a", 2, 3, 1),
     ("a", 1, 4, 1), ("a", 1, 4, 0), ("a", 0, 4, 0), ("pair", 2, 0), ("zsum", 1), ("a", 0, 4, 1), ("zsum", 7),
-    ("b", 3, 1), ("b", 3, 0), ("a", 2, 4, 0), ("zsum", 0), ("a", 2, 4, 1), ("sent",), ("end",), ("b", 4, 1),
-    ("b", 4, 0),
+    ("b", 3, 1), ("b", 3, 0), ("a", 2, 4, 0), ("zsum", 0), ("a", 2, 4, 1), ("sent",), ("end",), ("sent", 6),
+    ("b", 4, 1), ("b", 4, 0),
 )
 
 
@@ -293,10 +293,10 @@
             mean = jnp.where(member[k], cross, 0.0) / sizes[k]
             loss[k] = jnp.sum(mean)
 
-    def sent():
-        for copy in waits[:-16]:
+    def sent(kept=16):
+        for copy in waits[:-kept]:
             copy.wait_send()
-        del waits[:-16]
+        del waits[:-kept]
 
     steps = {"product": product, "swap": swap, "pair": pair, "a": a, "zsum": zsum, "b": b, "end": end,
              "hits_x": hits_x, "hits_z": hits_z, "loss": finish_loss, "sent": sent}

time: 60 us -> 60 us (level)
  no operation moved by 1% of the time
where the time goes in v6:
time: 60 us; the launch traced here: 59.7 us
  Pallas kernels  57.8 us (96%)
  local copies, waits for them, and re-layouts  1.19 us (2%)
  between operations  0.64 us (1%)
    pallas_call x1, Pallas kernels, on_device(): pl.pallas_call(kernel, out_shape=(jax.ShapeDtypeStruct((vocab_rows // (NZ...  57.8 us

profile of v6, /device:TPU:1, one launch (start us, length us, event | category | flops | bytes accessed | tf_op | source)
XLA Modules:
  0.0 59.7 jit_solution(10619526857540935250)
XLA Ops:
  0.6 57.8 %head_gradient.1 = (f32[18,2048]{1,0:T(8,128)S(1)}, f32[4]{0:T(128)S(1)}) custom-call(bf16[640,2048]{1,0:T(8,128)(2,1)} %hidden_hbm.1, bf16[864,2048]{1,0:T(8,128)(2,1)} %head_hbm.1, s32[640]{0:T(1024)} %targets_hbm.1, s32[4]{0:T(128)} %counts_hbm.1, s32[4]{0:T(128)} %lengths_hbm.1), custom_call_target="tpu_custom_call" | custom-call | flops 4529848320 | bytes 6160384 | tf_op jit(solution)/shard_map/head_gradient/pallas_call | solution.py:328
  58.5 0.5 copy.9
  59.0 0.7 %copy.10 = f32[18,2048]{1,0:T(8,128)} copy(f32[18,2048]{1,0:T(8,128)S(1)} %get-tuple-element.9) | data formatting | bytes 294912
